TPU v7x, 32 devices: a whole 2x2x4 slice. The times are simulated.
32 devices in a mesh: blk: 4 (over y, x), tile: 8 (over z, core).
Axes of the slice: x: 2, y: 2, z: 4, core: 2. Of those that a mesh axis runs over, the one named last changes fastest.
Arguments:
- grid_feat: bfloat16 [8192, 512], P(('blk', 'tile')), may hold values from -18 to 18
- queries: bfloat16 [8192, 512], P(('blk', 'tile')), may hold values from -90 to 90
- obs_keys: bfloat16 [256, 512], P(('blk', 'tile')), may hold values from -4 to 4
- obs_values: bfloat16 [256, 512], P(('blk', 'tile')), may hold values from -6 to 6
- block_mask: int32 [64, 2], P(('blk', 'tile')), may hold values from 0 to 1, as said below
- obs_valid: int32 [2], replicated, may hold values from 2 to 128, as said below
- out_weight: bfloat16 [512, 512], replicated, may hold values from -0.25 to 0.25
- conv_weight: bfloat16 [3, 3, 512, 512], replicated, may hold values from -0.09375 to 0.09375
Outputs:
- layer_out: bfloat16 [8192, 512], P(('blk', 'tile'))
Inputs may be any that keep to these rules, and one draw needn't show every extreme that they name: `block_mask`: row t has a 1 in column t mod 2. `obs_valid`: at least one entry equals 128.
All inputs are finite; a program needn't handle non-finite values.
Results may differ from a plain program's by a relative error of at most 0.007.
Values may be sent and summed in bfloat16 or wider, within the bound.
No kernel may reach another device: no remote copies, remote signals or barrier semaphores. Data moves between devices by JAX's collectives and lax.ppermute only.
A program may use at most 64 MiB of HBM per device.

v0:
```python
import functools
import math

import jax
import jax.numpy as jnp
from jax import lax
from jax.experimental import pallas as pl
from jax.experimental.pallas import tpu as pltpu
from jax.sharding import PartitionSpec as P

HEADS = 8
OBS_BLOCK = 128
AXES = ("blk", "tile")
PAIR = 2
CORES = 2
NT = (((1,), (1,)), ((), ()))


def attend_kernel(
    tiles, lon, width, nblocks, rows,
    meta_ref, same_ref, other_ref, *refs,
):
    queries_refs, grid_refs = refs[:tiles], refs[tiles : 2 * tiles]
    out_weight_refs = refs[2 * tiles : 2 * tiles + 2]
    hidden_ref, near_ref, far_ref, mixed_ref = refs[2 * tiles + 2 :]
    head = width // HEADS
    pair = PAIR * head
    obs = nblocks * OBS_BLOCK
    scale = head ** (-0.5) * math.log2(math.e)

    core = meta_ref[0]
    half = OBS_BLOCK // CORES
    key_lane = lax.broadcasted_iota(jnp.int32, (1, OBS_BLOCK), 1)
    spread = (key_lane % half) // rows * (CORES * rows) + key_lane % rows
    first = key_lane < half

    def limit(tile, block):
        allowed = meta_ref[1 + (1 + tile) * nblocks + block] > 0
        return jnp.where(allowed, meta_ref[1 + block], 0)

    def row_bias(tile):
        parts = []
        for parity in (core, 1 - core):
            place = spread + parity * rows
            for block in range(0, nblocks, CORES):
                end = jnp.where(first, limit(tile, block), limit(tile, block + 1))
                parts.append(jnp.where(place < end, 0.0, -jnp.inf))
        return jnp.concatenate(parts, axis=1)

    biases = [row_bias(t) for t in range(tiles)]

    lane = lax.broadcasted_iota(jnp.int32, (obs, pair), 1)
    ones = [(lane // head == h).astype(jnp.bfloat16) for h in range(PAIR)]

    def both_cores(cols):
        parts = [ref[:, :, cols].reshape(obs // CORES, pair) for ref in (same_ref, other_ref)]
        return jnp.concatenate(parts, axis=0)

    for group in range(HEADS // PAIR):
        cols = slice(group * pair, (group + 1) * pair)
        keys = both_cores(cols)
        values = both_cores(slice(width + group * pair, width + (group + 1) * pair))
        key_parts = [keys * one for one in ones]
        value_parts = jnp.concatenate(
            [jnp.concatenate([values * one, one], axis=1) for one in ones], axis=0
        )
        query = jnp.concatenate([ref[:, cols] for ref in queries_refs], axis=0)
        weights = []
        for part in key_parts:
            scores = lax.dot_general(query, part, NT, preferred_element_type=jnp.float32)
            pieces = []
            for t, bias in enumerate(biases):
                piece = scores[t * lon : (t + 1) * lon] * scale + bias
                top = jnp.max(piece, axis=1, keepdims=True)
                pieces.append(jnp.exp2(piece - top).astype(jnp.bfloat16))
            weights.append(jnp.concatenate(pieces, axis=0))
        both = jnp.dot(
            jnp.concatenate(weights, axis=1), value_parts, preferred_element_type=jnp.float32
        )
        mixed_ref[:, cols] = (both[:, :pair] / both[:, pair:]).astype(jnp.bfloat16)

    depth = width // len(out_weight_refs)
    projected = sum(
        jnp.dot(
            mixed_ref[:, i * depth : (i + 1) * depth], ref[...], preferred_element_type=jnp.float32
        )
        for i, ref in enumerate(out_weight_refs)
    )
    normed = []
    for t, ref in enumerate(grid_refs):
        here = slice(t * lon, (t + 1) * lon)
        hidden = (ref[...].astype(jnp.float32) + projected[here]).astype(jnp.bfloat16)
        hidden_ref[here, :] = hidden
        wide = hidden.astype(jnp.float32)
        normed.append(wide * lax.rsqrt(jnp.mean(wide * wide, axis=-1, keepdims=True) + 1e-06))
    near_ref[...] = jnp.where(core == 0, normed[-1], normed[0]).astype(jnp.bfloat16)
    far_ref[...] = jnp.where(core == 0, normed[0], normed[-1]).astype(jnp.bfloat16)


def convolve_kernel(
    tiles, lon,
    meta_ref, near_ref, far_ref, near_sent_ref, far_sent_ref, hidden_ref, *refs,
):
    conv_refs = refs[:3]
    out_ref, field_ref = refs[3:]
    core = meta_ref[0]
    for k, ref in enumerate((near_ref, near_sent_ref, far_sent_ref, far_ref)):
        place = jnp.where(core == 0, tiles + 1 - k, k) * lon
        field_ref[pl.ds(pl.multiple_of(place, lon), lon), :] = ref[...]
    sums = [None, None, None]
    for lat_off in range(3):
        moved = field_ref[lat_off * lon : (lat_off + tiles) * lon, :]
        for lon_off in range(3):
            term = jnp.dot(
                moved, conv_refs[lat_off][lon_off], preferred_element_type=jnp.float32
            )
            sums[lon_off] = term if sums[lon_off] is None else sums[lon_off] + term
    for t in range(tiles):
        here = slice(t * lon, (t + 1) * lon)
        out_ref[here, :] = (
            hidden_ref[here, :].astype(jnp.float32)
            + pltpu.roll(sums[0][here], 1, 0)
            + sums[1][here]
            + pltpu.roll(sums[2][here], lon - 1, 0)
        ).astype(jnp.bfloat16)


def on_device(
    grid_feat, queries, obs_keys, obs_values, block_mask, obs_valid, out_weight, conv_weight
):
    q_dev, width = queries.shape
    tiles, nblocks = block_mask.shape
    rows = obs_keys.shape[0]
    lon = q_dev // tiles
    obs = nblocks * OBS_BLOCK
    devices = lax.axis_size(AXES)
    pairs = devices // CORES
    core = lax.axis_index(AXES) % CORES

    block = jnp.concatenate([obs_keys, obs_values], axis=1)
    groups = [list(range(c, devices, CORES)) for c in range(CORES)]
    same = lax.all_to_all(
        jnp.broadcast_to(block[None], (pairs,) + block.shape), AXES, 0, 0, axis_index_groups=groups
    )
    swap = [(i, i ^ 1) for i in range(devices)]
    across = [(i, i + 1) for i in range(1, devices - 1, CORES)]
    across += [(target, source) for source, target in across]
    other = lax.ppermute(same, AXES, swap)

    def pieces(array, count):
        return jnp.split(array, count, axis=0)

    query_rows, grid_rows, weight_rows, conv_rows = lax.optimization_barrier(
        (
            pieces(queries, tiles),
            pieces(grid_feat, tiles),
            pieces(out_weight, 2),
            [conv_weight[i] for i in range(3)],
        )
    )
    meta = jnp.concatenate([core.astype(jnp.int32)[None], obs_valid, block_mask.reshape(-1)])

    vmem = pl.BlockSpec(memory_space=pltpu.VMEM)
    smem = pl.BlockSpec(memory_space=pltpu.SMEM)
    row_shape = jax.ShapeDtypeStruct((lon, width), jnp.bfloat16)
    full_shape = jax.ShapeDtypeStruct((q_dev, width), jnp.bfloat16)
    hidden, near_sent, far_sent = pl.pallas_call(
        functools.partial(attend_kernel, tiles, lon, width, nblocks, rows),
        out_shape=[full_shape, row_shape, row_shape],
        in_specs=[smem] + [vmem] * (4 + 2 * tiles),
        out_specs=[vmem] * 3,
        scratch_shapes=[pltpu.VMEM((q_dev, width), jnp.bfloat16)],
        compiler_params=pltpu.CompilerParams(vmem_limit_bytes=40 * 2**20),
        cost_estimate=pl.CostEstimate(
            flops=2 * q_dev * width * (width + 4 * obs), bytes_accessed=q_dev * width * 8, transcendentals=0
        ),
        name="attend",
    )(meta, same, other, *query_rows, *grid_rows, *weight_rows)
    far = lax.ppermute(far_sent, AXES, across)
    near = lax.ppermute(near_sent, AXES, swap)
    return pl.pallas_call(
        functools.partial(convolve_kernel, tiles, lon),
        out_shape=full_shape,
        in_specs=[smem] + [vmem] * 8,
        out_specs=vmem,
        scratch_shapes=[pltpu.VMEM(((tiles + 2) * lon, width), jnp.bfloat16)],
        compiler_params=pltpu.CompilerParams(vmem_limit_bytes=40 * 2**20),
        cost_estimate=pl.CostEstimate(
            flops=18 * q_dev * width * width, bytes_accessed=2 * conv_weight.size, transcendentals=0
        ),
        name="convolve",
    )(meta, near, far, near_sent, far_sent, hidden, *conv_rows)


def solution(mesh):
    in_specs = (
        P(AXES, None),
        P(AXES, None),
        P(AXES, None),
        P(AXES, None),
        P(AXES, None),
        P(),
        P(),
        P(),
    )
    return jax.shard_map(
        on_device, mesh=mesh, in_specs=in_specs, out_specs=P(AXES, None), check_vma=False
    )
```

profile of v0, /device:TPU:4, one launch (start us, length us, event | category | flops | bytes accessed | tf_op | source)
XLA Modules:
  0.0 40.1 jit_solution(2101582177045823224)
XLA Ops:
  0.0 0.7 %pad_maximum_fusion = bf16[8,1024]{1,0:T(8,128)(2,1)S(1)} fusion(bf16[8,512]{1,0:T(8,128)(2,1)} %param.11, bf16[8,512]{1,0:T(8,128)(2,1)} %param.10), kind=kLoop, calls=%fused_computation.3 | loop fusion | flops 32768 | bytes 32768 | tf_op jit(solution)/shard_map/concatenate | solution.py:140
  0.7 0.7 %broadcast_in_dim.10 = bf16[16,8,1024]{2,1,0:T(8,128)(2,1)} broadcast(bf16[8,1024]{1,0:T(8,128)(2,1)S(1)} %pad_maximum_fusion), dimensions={1,2} | broadcast | bytes 278528 | tf_op jit(solution)/shard_map/broadcast_in_dim | solution.py:143
  1.5 7.3 %all-to-all-start = ((bf16[16,8,1024]{2,1,0:T(8,128)(2,1)}), bf16[16,8,1024]{2,1,0:T(8,128)(2,1)S(1)}, u32[]{:S(2)}, u32[]{:S(2)}) async-start(bf16[16,8,1024]{2,1,0:T(8,128)(2,1)} %broadcast_in_dim.10), calls=%async_computation | async-start | bytes 524288 | tf_op jit(solution)/shard_map/all_to_all | solution.py:142
  8.7 1.9 %fusion = (bf16[256,512]{1,0:T(8,128)(2,1)}, bf16[256,512]{1,0:T(8,128)(2,1)}) fusion(bf16[512,512]{1,0:T(8,128)(2,1)} %param.14), kind=kLoop, calls=%fused_computation.5 | loop fusion | bytes 1048576 | tf_op jit(solution)/shard_map/split | solution.py:151
  10.6 0.0 copy-done.7
  10.6 0.1 reshape.4
  10.7 4.0 %slice_bitcast_fusion = (bf16[3,512,512]{2,1,0:T(8,128)(2,1)S(1)}, bf16[3,512,512]{2,1,0:T(8,128)(2,1)S(1)}, bf16[3,512,512]{2,1,0:T(8,128)(2,1)}) fusion(bf16[3,3,512,512]{3,2,1,0:T(8,128)(2,1)} %param.15), kind=kLoop, calls=%fused_computation | loop fusion | bytes 9437184 | tf_op jit(solution)/shard_map/squeeze | solution.py:158
  14.7 3.2 %all-to-all-done.same_ref = bf16[16,8,1024]{2,1,0:T(8,128)(2,1)S(1)} async-done(((bf16[16,8,1024]{2,1,0:T(8,128)(2,1)}), bf16[16,8,1024]{2,1,0:T(8,128)(2,1)S(1)}, u32[]{:S(2)}, u32[]{:S(2)}) %all-to-all-start) | async-done | bytes 262176 | tf_op jit(solution)/shard_map/all_to_all | solution.py:142
  17.9 0.0 collective-permute-start
  18.0 1.8 %fusion.1 = (bf16[128,512]{1,0:T(8,128)(2,1)S(1)}, bf16[128,512]{1,0:T(8,128)(2,1)}, bf16[128,512]{1,0:T(8,128)(2,1)}, bf16[128,512]{1,0:T(8,128)(2,1)}) fusion(bf16[256,512]{1,0:T(8,128)(2,1)} %param.8, bf16[256,512]{1,0:T(8,128)(2,1)} %param.9), kind=kLoop, calls=%fused_computation.6 | loop fusion | bytes 1048576 | tf_op jit(solution)/shard_map/split | solution.py:151
  19.8 0.1 pad_add_fusion.meta_ref
  19.9 0.0 collective-permute-done.other_ref
  19.9 1.1 %copy-done.1 = bf16[256,512]{1,0:T(8,128)(2,1)S(1)} copy-done((bf16[256,512]{1,0:T(8,128)(2,1)S(1)}, bf16[256,512]{1,0:T(8,128)(2,1)}, u32[]{:S(2)}) %copy-start.1) | copy-done | bytes 262168
  20.9 0.9 %copy-done.2 = bf16[256,512]{1,0:T(8,128)(2,1)S(1)} copy-done((bf16[256,512]{1,0:T(8,128)(2,1)S(1)}, bf16[256,512]{1,0:T(8,128)(2,1)}, u32[]{:S(2)}) %copy-start.2) | copy-done | bytes 262168
  21.9 0.9 %copy-done.3 = bf16[128,512]{1,0:T(8,128)(2,1)S(1)} copy-done((bf16[128,512]{1,0:T(8,128)(2,1)S(1)}, bf16[128,512]{1,0:T(8,128)(2,1)}, u32[]{:S(2)}) %copy-start.3) | copy-done | bytes 131096
  22.8 0.9 %copy-done.4 = bf16[128,512]{1,0:T(8,128)(2,1)S(1)} copy-done((bf16[128,512]{1,0:T(8,128)(2,1)S(1)}, bf16[128,512]{1,0:T(8,128)(2,1)}, u32[]{:S(2)}) %copy-start.4) | copy-done | bytes 131096
  23.7 0.9 %copy-done.5 = bf16[128,512]{1,0:T(8,128)(2,1)S(1)} copy-done((bf16[128,512]{1,0:T(8,128)(2,1)S(1)}, bf16[128,512]{1,0:T(8,128)(2,1)}, u32[]{:S(2)}) %copy-start.5) | copy-done | bytes 131096
  24.6 2.4 %attend.1 = (bf16[256,512]{1,0:T(8,128)(2,1)S(1)}, bf16[128,512]{1,0:T(8,128)(2,1)S(1)}, bf16[128,512]{1,0:T(8,128)(2,1)S(1)}) custom-call(s32[7]{0:T(128)S(1)} %pad_add_fusion.meta_ref, bf16[16,8,1024]{2,1,0:T(8,128)(2,1)S(1)} %all-to-all-done.same_ref, bf16[16,8,1024]{2,1,0:T(8,128)(2,1)} %collective-permute-done.other_ref, ...), custom_call_target="tpu_custom_call" | custom-call | flops 402653184 | bytes 1048576 | tf_op jit(solution)/shard_map/attend/pallas_call | solution.py:167
  27.0 0.6 %collective-permute-start.1 = (bf16[128,512]{1,0:T(8,128)(2,1)S(1)}, bf16[128,512]{1,0:T(8,128)(2,1)S(1)}, u32[]{:S(2)}, u32[]{:S(2)}) collective-permute-start(bf16[128,512]{1,0:T(8,128)(2,1)S(1)} %get-tuple-element.23.near_sent_ref), channel_id=1, source_target_pairs={{0,1},{1,0},{2,3},{3,2},{4,5},{5,4},{6,7},{7,6},{8,9},{9,8},{10,11... | collective-permute-start | bytes 393224 | tf_op jit(solution)/shard_map/ppermute | solution.py:180
  27.6 3.0 %collective-permute-start.2 = (bf16[128,512]{1,0:T(8,128)(2,1)S(1)}, bf16[128,512]{1,0:T(8,128)(2,1)S(1)}, u32[]{:S(2)}, u32[]{:S(2)}) collective-permute-start(bf16[128,512]{1,0:T(8,128)(2,1)S(1)} %get-tuple-element.24.far_sent_ref), channel_id=1, source_target_pairs={{1,2},{3,4},{5,6},{7,8},{9,10},{11,12},{13,14},{15,16},{17,18},{19... | collective-permute-start | bytes 393224 | tf_op jit(solution)/shard_map/ppermute | solution.py:179
  30.6 0.0 collective-permute-done.1.near_ref
  30.6 6.9 %collective-permute-done.2.far_ref = bf16[128,512]{1,0:T(8,128)(2,1)S(1)} collective-permute-done((bf16[128,512]{1,0:T(8,128)(2,1)S(1)}, bf16[128,512]{1,0:T(8,128)(2,1)S(1)}, u32[]{:S(2)}, u32[]{:S(2)}) %collective-permute-start.2) | collective-permute-done | bytes 131104 | tf_op jit(solution)/shard_map/ppermute | solution.py:179
  37.4 0.0 copy-done
  37.4 2.7 %convolve.1 = bf16[256,512]{1,0:T(8,128)(2,1)} custom-call(s32[7]{0:T(128)S(1)} %pad_add_fusion.meta_ref, bf16[128,512]{1,0:T(8,128)(2,1)S(1)} %collective-permute-done.1.near_ref, bf16[128,512]{1,0:T(8,128)(2,1)S(1)} %collective-permute-done.2.far_ref, bf16[128,512]{1,0:T(8,128)(2,1)S(1)} %get-tuple-element.23.near_sent_ref, ...), custom_call_target="tpu_custom_call" | custom-call | flops 1207959552 | bytes 4718592 | tf_op jit(solution)/shard_map/convolve/pallas_call | solution.py:181
  (9 shorter events, 0.0 us)
Async XLA Ops:
  0.0 10.6 %copy-start.7 = (s32[2,2]{1,0:T(2,128)S(1)}, s32[2,2]{1,0:T(2,128)}, u32[]{:S(2)}) copy-start(s32[2,2]{1,0:T(2,128)} %param.12) | copy-start | bytes 52
  1.5 16.5 %all-to-all-start = ((bf16[16,8,1024]{2,1,0:T(8,128)(2,1)}), bf16[16,8,1024]{2,1,0:T(8,128)(2,1)S(1)}, u32[]{:S(2)}, u32[]{:S(2)}) async-start(bf16[16,8,1024]{2,1,0:T(8,128)(2,1)} %broadcast_in_dim.10), calls=%async_computation | async-start | bytes 524288 | tf_op jit(solution)/shard_map/all_to_all | solution.py:142
  10.7 9.1 %copy-start.6 = (s32[2]{0:T(128)S(1)}, s32[2]{0:T(128)}, u32[]{:S(2)}) copy-start(s32[2]{0:T(128)} %param.13) | copy-start | bytes 28
  17.9 1.9 %collective-permute-start = (bf16[16,8,1024]{2,1,0:T(8,128)(2,1)S(1)}, bf16[16,8,1024]{2,1,0:T(8,128)(2,1)}, u32[]{:S(2)}, u32[]{:S(2)}) collective-permute-start(bf16[16,8,1024]{2,1,0:T(8,128)(2,1)S(1)} %all-to-all-done.same_ref), channel_id=1, source_target_pairs={{0,1},{1,0},{2,3},{3,2},{4,5},{5,4},{6,7},{7,6},{8,9},{9,8},{10,11... | collective-permute-start | bytes 786440 | tf_op jit(solution)/shard_map/ppermute | solution.py:148
  19.8 17.7 %copy-start = (bf16[3,512,512]{2,1,0:T(8,128)(2,1)S(1)}, bf16[3,512,512]{2,1,0:T(8,128)(2,1)}, u32[]{:S(2)}) copy-start(bf16[3,512,512]{2,1,0:T(8,128)(2,1)} %get-tuple-element.27.refs_1_) | copy-start | bytes 4718596
  19.9 1.1 %copy-start.1 = (bf16[256,512]{1,0:T(8,128)(2,1)S(1)}, bf16[256,512]{1,0:T(8,128)(2,1)}, u32[]{:S(2)}) copy-start(bf16[256,512]{1,0:T(8,128)(2,1)} %get-tuple-element.22.refs_5_) | copy-start | bytes 786436
  20.9 0.9 %copy-start.2 = (bf16[256,512]{1,0:T(8,128)(2,1)S(1)}, bf16[256,512]{1,0:T(8,128)(2,1)}, u32[]{:S(2)}) copy-start(bf16[256,512]{1,0:T(8,128)(2,1)} %get-tuple-element.21.refs_4_) | copy-start | bytes 786436
  21.9 0.9 %copy-start.3 = (bf16[128,512]{1,0:T(8,128)(2,1)S(1)}, bf16[128,512]{1,0:T(8,128)(2,1)}, u32[]{:S(2)}) copy-start(bf16[128,512]{1,0:T(8,128)(2,1)} %get-tuple-element.19.refs_2_) | copy-start | bytes 393220
  22.8 0.9 %copy-start.4 = (bf16[128,512]{1,0:T(8,128)(2,1)S(1)}, bf16[128,512]{1,0:T(8,128)(2,1)}, u32[]{:S(2)}) copy-start(bf16[128,512]{1,0:T(8,128)(2,1)} %get-tuple-element.17.refs_0_) | copy-start | bytes 393220
  23.7 0.9 %copy-start.5 = (bf16[128,512]{1,0:T(8,128)(2,1)S(1)}, bf16[128,512]{1,0:T(8,128)(2,1)}, u32[]{:S(2)}) copy-start(bf16[128,512]{1,0:T(8,128)(2,1)} %get-tuple-element.18.refs_1_) | copy-start | bytes 393220
  27.0 3.6 %collective-permute-start.1 = (bf16[128,512]{1,0:T(8,128)(2,1)S(1)}, bf16[128,512]{1,0:T(8,128)(2,1)S(1)}, u32[]{:S(2)}, u32[]{:S(2)}) collective-permute-start(bf16[128,512]{1,0:T(8,128)(2,1)S(1)} %get-tuple-element.23.near_sent_ref), channel_id=1, source_target_pairs={{0,1},{1,0},{2,3},{3,2},{4,5},{5,4},{6,7},{7,6},{8,9},{9,8},{10,11... | collective-permute-start | bytes 393224 | tf_op jit(solution)/shard_map/ppermute | solution.py:180
  27.6 9.9 %collective-permute-start.2 = (bf16[128,512]{1,0:T(8,128)(2,1)S(1)}, bf16[128,512]{1,0:T(8,128)(2,1)S(1)}, u32[]{:S(2)}, u32[]{:S(2)}) collective-permute-start(bf16[128,512]{1,0:T(8,128)(2,1)S(1)} %get-tuple-element.24.far_sent_ref), channel_id=1, source_target_pairs={{1,2},{3,4},{5,6},{7,8},{9,10},{11,12},{13,14},{15,16},{17,18},{19... | collective-permute-start | bytes 393224 | tf_op jit(solution)/shard_map/ppermute | solution.py:179
where the time goes:
time: 40.5 us; the launch traced here: 40.1 us
  local copies, waits for them, and re-layouts  13.2 us (33%)
  starting transfers between devices  10.8 us (27%)
  waiting for transfers between devices  10.1 us (25%)
  Pallas kernels  5.07 us (13%)
  other arithmetic  0.8 us (2%)
    all_to_all x1, starting transfers between devices, on_device(): lax.all_to_all(jnp.broadcast_to(block[None], (pairs,) + block.shape), AXE...  7.28 us
    ppermute x1, waiting for transfers between devices, on_device(): far = lax.ppermute(far_sent, AXES, across)  6.86 us
    unnamed x16, local copies, waits for them, and re-layouts  4.73 us
    squeeze x1, local copies, waits for them, and re-layouts, on_device(): conv_weight[i]  4.01 us
    split x2, local copies, waits for them, and re-layouts, pieces(): return jnp.split(array, count, axis=0)  3.7 us
    all_to_all x1, waiting for transfers between devices, on_device(): lax.all_to_all(jnp.broadcast_to(block[None], (pairs,) + block.shape), AXE...  3.25 us
    ppermute x1, starting transfers between devices, on_device(): far = lax.ppermute(far_sent, AXES, across)  2.99 us
    pallas_call x1, Pallas kernels, on_device(): pl.pallas_call(functools.partial(convolve_kernel, tiles, lon), out_shape=...  2.67 us
  transfers between devices with their start and end apart: 4, of which 2 were waited for; matrix products, arithmetic and copies ran while one was open for 20% of the time, Pallas kernels for 0%

commit v1 on v0

v1 whole, which is shorter than its diff:
```python
import functools
import math

import jax
import jax.numpy as jnp
from jax import lax
from jax.experimental import pallas as pl
from jax.experimental.pallas import tpu as pltpu
from jax.sharding import PartitionSpec as P

HEADS = 8
OBS_BLOCK = 128
AXES = ("blk", "tile")
PAIR = 2
CORES = 2
MASK_ROWS = 16
NT = (((1,), (1,)), ((), ()))


def attend(lon, width, nblocks, rows, core, valid, row_refs, same_ref, other_ref, weight_refs, mixed_ref):
    head = width // HEADS
    pair = PAIR * head
    obs = nblocks * OBS_BLOCK
    scale = head ** (-0.5) * math.log2(math.e)
    half = OBS_BLOCK // CORES
    key_lane = lax.broadcasted_iota(jnp.int32, (1, OBS_BLOCK), 1)
    spread = (key_lane % half) // rows * (CORES * rows) + key_lane % rows
    first = key_lane < half

    def row_bias(ref):
        mask = ref[2 * lon : 2 * lon + MASK_ROWS, :].astype(jnp.float32)[:1]

        def limit(block):
            allowed = jnp.broadcast_to(mask[:, block : block + 1], (1, OBS_BLOCK)) > 0.5
            return jnp.where(allowed, valid(block), 0)

        parts = []
        for parity in (core, 1 - core):
            place = spread + parity * rows
            for block in range(0, nblocks, CORES):
                end = jnp.where(first, limit(block), limit(block + 1))
                parts.append(jnp.where(place < end, 0.0, -jnp.inf))
        return jnp.concatenate(parts, axis=1)

    biases = [row_bias(ref) for ref in row_refs]
    lane = lax.broadcasted_iota(jnp.int32, (obs, pair), 1)
    ones = [(lane // head == h).astype(jnp.bfloat16) for h in range(PAIR)]

    def both_cores(cols):
        parts = [ref[:, :, cols].reshape(obs // CORES, pair) for ref in (same_ref, other_ref)]
        return jnp.concatenate(parts, axis=0)

    for group in range(HEADS // PAIR):
        cols = slice(group * pair, (group + 1) * pair)
        keys = both_cores(cols)
        values = both_cores(slice(width + group * pair, width + (group + 1) * pair))
        key_parts = [keys * one for one in ones]
        value_parts = jnp.concatenate(
            [jnp.concatenate([values * one, one], axis=1) for one in ones], axis=0
        )
        query = jnp.concatenate([ref[:lon, cols] for ref in row_refs], axis=0)
        weights = []
        for part in key_parts:
            scores = lax.dot_general(query, part, NT, preferred_element_type=jnp.float32)
            pieces = []
            for t, bias in enumerate(biases):
                piece = scores[t * lon : (t + 1) * lon] * scale + bias
                top = jnp.max(piece, axis=1, keepdims=True)
                pieces.append(jnp.exp2(piece - top).astype(jnp.bfloat16))
            weights.append(jnp.concatenate(pieces, axis=0))
        both = jnp.dot(
            jnp.concatenate(weights, axis=1), value_parts, preferred_element_type=jnp.float32
        )
        mixed_ref[:, cols] = (both[:, :pair] / both[:, pair:]).astype(jnp.bfloat16)

    depth = width // len(weight_refs)
    projected = sum(
        jnp.dot(
            mixed_ref[:, i * depth : (i + 1) * depth], ref[...], preferred_element_type=jnp.float32
        )
        for i, ref in enumerate(weight_refs)
    )
    grid = jnp.concatenate([ref[lon : 2 * lon, :] for ref in row_refs], axis=0)
    wide = (grid.astype(jnp.float32) + projected).astype(jnp.bfloat16).astype(jnp.float32)
    normed = wide * lax.rsqrt(jnp.mean(wide * wide, axis=-1, keepdims=True) + 1e-06)
    return wide, normed


def around(parts, lon):
    return pltpu.roll(parts[0], 1, 0) + parts[1] + pltpu.roll(parts[2], lon - 1, 0)


def inner_kernel(
    lon, width, nblocks, rows,
    meta_ref, near_ref, near_sent_ref, far_sent_ref, same_ref, other_ref, upper_ref, lower_ref,
    conv_hbm, done_ref, partial_ref, conv_ref, mixed_ref, field_ref, sems,
):
    core = meta_ref[0]
    copies = [
        pltpu.make_async_copy(conv_hbm.at[source], conv_ref.at[i], sems.at[i])
        for i, source in enumerate((1, 2 - 2 * core, 2 * core))
    ]
    for copy in copies:
        copy.start()
    wide, normed = attend(
        lon, width, nblocks, rows, core, lambda block: meta_ref[2 + block],
        (near_ref, near_sent_ref, far_sent_ref), same_ref, other_ref, (upper_ref, lower_ref), mixed_ref,
    )
    field_ref[...] = normed.astype(jnp.bfloat16)
    for copy in copies:
        copy.wait()
    inputs = jnp.concatenate([field_ref[lon:, :], field_ref[: 2 * lon, :]], axis=1)
    full, open_end = [], []
    for lon_off in range(3):
        taps = conv_ref[:2, lon_off].reshape(2 * width, width)
        term = jnp.dot(inputs, taps, preferred_element_type=jnp.float32)
        full.append(
            term[:lon]
            + jnp.dot(field_ref[2 * lon :, :], conv_ref[2, lon_off], preferred_element_type=jnp.float32)
        )
        open_end.append(term[lon:])
    done_ref[...] = (wide[lon : 2 * lon] + around(full, lon)).astype(jnp.bfloat16)
    partial_ref[...] = wide[2 * lon :] + around(open_end, lon)


def outer_kernel(
    lon, width, nblocks, rows,
    meta_ref, far_ref, same_ref, other_ref, upper_ref, lower_ref, done_ref, partial_ref,
    conv_hbm, out_ref, conv_ref, mixed_ref, sem,
):
    core = meta_ref[0]
    copy = pltpu.make_async_copy(conv_hbm.at[2 * core], conv_ref, sem)
    copy.start()
    _, normed = attend(
        lon, width, nblocks, rows, core, lambda block: meta_ref[2 + block],
        (far_ref,), same_ref, other_ref, (upper_ref, lower_ref), mixed_ref,
    )
    field = jnp.where(meta_ref[1] > 0, normed, 0.0).astype(jnp.bfloat16)
    copy.wait()
    parts = [
        jnp.dot(field, conv_ref[lon_off], preferred_element_type=jnp.float32) for lon_off in range(3)
    ]
    last = (partial_ref[...] + around(parts, lon)).astype(jnp.bfloat16)
    out_ref[pl.ds(pl.multiple_of((1 - core) * lon, lon), lon), :] = done_ref[...]
    out_ref[pl.ds(pl.multiple_of(core * lon, lon), lon), :] = last


def on_device(
    grid_feat, queries, obs_keys, obs_values, block_mask, obs_valid, out_weight, conv_weight
):
    q_dev, width = queries.shape
    tiles, nblocks = block_mask.shape
    rows = obs_keys.shape[0]
    lon = q_dev // tiles
    obs = nblocks * OBS_BLOCK
    devices = lax.axis_size(AXES)
    pairs = devices // CORES
    me = lax.axis_index(AXES)
    core = me % CORES

    block = jnp.concatenate([obs_keys, obs_values], axis=1)
    groups = [list(range(c, devices, CORES)) for c in range(CORES)]
    same = lax.all_to_all(
        jnp.broadcast_to(block[None], (pairs,) + block.shape), AXES, 0, 0, axis_index_groups=groups
    )
    swap = [(i, i ^ 1) for i in range(devices)]
    across = [(i, i + 1) for i in range(1, devices - 1, CORES)]
    across += [(target, source) for source, target in across]

    query_rows, grid_rows = lax.optimization_barrier(
        (jnp.split(queries, tiles, axis=0), jnp.split(grid_feat, tiles, axis=0))
    )
    mask_tile = jnp.pad(block_mask.astype(jnp.bfloat16), ((0, 0), (0, width - nblocks)))

    def packed(tile):
        mask = jnp.broadcast_to(mask_tile[tile][None], (MASK_ROWS, width))
        return jnp.concatenate([query_rows[tile], grid_rows[tile], mask], axis=0)

    first, last = packed(0), packed(tiles - 1)
    far_sent = jnp.where(core == 0, first, last)
    near_sent = jnp.where(core == 0, last, first)
    far = lax.ppermute(far_sent, AXES, across)
    near = lax.ppermute(near_sent, AXES, swap)
    other = lax.ppermute(same, AXES, swap)
    out_weight, _ = lax.optimization_barrier((out_weight, same))
    upper, lower = lax.optimization_barrier(tuple(jnp.split(out_weight, 2, axis=0)))

    far_exists = (me > 0) & (me < devices - 1)
    meta = jnp.concatenate([jnp.stack([core, far_exists.astype(core.dtype)]).astype(jnp.int32), obs_valid])

    vmem = pl.BlockSpec(memory_space=pltpu.VMEM)
    smem = pl.BlockSpec(memory_space=pltpu.SMEM)
    hbm = pl.BlockSpec(memory_space=pltpu.HBM)
    sizes = (lon, width, nblocks, rows)
    params = pltpu.CompilerParams(vmem_limit_bytes=48 * 2**20)
    tap_flops, row_flops = 2 * lon * width * width, 2 * lon * width * (width + 4 * obs)
    done, partial = pl.pallas_call(
        functools.partial(inner_kernel, *sizes),
        out_shape=[
            jax.ShapeDtypeStruct((lon, width), jnp.bfloat16),
            jax.ShapeDtypeStruct((lon, width), jnp.float32),
        ],
        in_specs=[smem] + [vmem] * 7 + [hbm],
        out_specs=[vmem] * 2,
        scratch_shapes=[
            pltpu.VMEM(conv_weight.shape, jnp.bfloat16),
            pltpu.VMEM((3 * lon, width), jnp.bfloat16),
            pltpu.VMEM((3 * lon, width), jnp.bfloat16),
            pltpu.SemaphoreType.DMA((3,)),
        ],
        compiler_params=params,
        cost_estimate=pl.CostEstimate(
            flops=3 * row_flops + 15 * tap_flops, bytes_accessed=2 * conv_weight.size, transcendentals=0
        ),
        name="inner",
    )(meta, near, near_sent, far_sent, same, other, upper, lower, conv_weight)
    return pl.pallas_call(
        functools.partial(outer_kernel, *sizes),
        out_shape=jax.ShapeDtypeStruct((q_dev, width), jnp.bfloat16),
        in_specs=[smem] + [vmem] * 7 + [hbm],
        out_specs=vmem,
        scratch_shapes=[
            pltpu.VMEM(conv_weight.shape[1:], jnp.bfloat16),
            pltpu.VMEM((lon, width), jnp.bfloat16),
            pltpu.SemaphoreType.DMA,
        ],
        compiler_params=params,
        cost_estimate=pl.CostEstimate(
            flops=row_flops + 3 * tap_flops, bytes_accessed=conv_weight.size, transcendentals=0
        ),
        name="outer",
    )(meta, far, same, other, upper, lower, done, partial, conv_weight)


def solution(mesh):
    in_specs = (
        P(AXES, None),
        P(AXES, None),
        P(AXES, None),
        P(AXES, None),
        P(AXES, None),
        P(),
        P(),
        P(),
    )
    return jax.shard_map(
        on_device, mesh=mesh, in_specs=in_specs, out_specs=P(AXES, None), check_vma=False
    )
```

time: 40.5 us -> 31.7 us (0.78)
  the two profiles are of different devices: /device:TPU:4 before, /device:TPU:0 now
where the time goes in v1:
time: 31.7 us; the launch traced here: 31.2 us
  starting transfers between devices  9.06 us (29%)
  Pallas kernels  8.94 us (28%)
  waiting for transfers between devices  7.92 us (25%)
  local copies, waits for them, and re-layouts  2.97 us (9%)
  other arithmetic  2.24 us (7%)
    all_to_all x1, starting transfers between devices, on_device(): lax.all_to_all(jnp.broadcast_to(block[None], (pairs,) + block.shape), AXE...  8.31 us
    all_to_all x1, waiting for transfers between devices, on_device(): lax.all_to_all(jnp.broadcast_to(block[None], (pairs,) + block.shape), AXE...  7.91 us
    pallas_call x1, Pallas kernels, on_device(): pl.pallas_call(functools.partial(inner_kernel, *sizes), out_shape=[jax.Sh...  5.19 us
    pallas_call x1, Pallas kernels, on_device(): pl.pallas_call(functools.partial(outer_kernel, *sizes), out_shape=jax.Sha...  3.76 us
    split x1, local copies, waits for them, and re-layouts, on_device(): jnp.split(grid_feat, tiles, axis=0)  1.13 us
    split x1, local copies, waits for them, and re-layouts, on_device(): jnp.split(out_weight, 2, axis=0)  1.06 us
    concatenate x1, other arithmetic, on_device(): jnp.concatenate([jnp.stack([core, far_exists.astype(core.dtype)]).astype(...  0.73 us
    broadcast_in_dim x1, local copies, waits for them, and re-layouts, on_device(): jnp.broadcast_to(block[None], (pairs,) + block.shape)  0.73 us
  transfers between devices with their start and end apart: 4, of which 1 were waited for; matrix products, arithmetic and copies ran while one was open for 12% of the time, Pallas kernels for 17%

profile of v1, /device:TPU:0, one launch (start us, length us, event | category | flops | bytes accessed | tf_op | source)
XLA Modules:
  0.0 31.2 jit_solution(8099420557763182721)
XLA Ops:
  0.0 0.7 %pad_maximum_fusion.2 = bf16[8,1024]{1,0:T(8,128)(2,1)S(1)} fusion(bf16[8,512]{1,0:T(8,128)(2,1)} %param.11, bf16[8,512]{1,0:T(8,128)(2,1)} %param.10), kind=kLoop, calls=%fused_computation.4 | loop fusion | flops 32768 | bytes 32768 | tf_op jit(solution)/shard_map/concatenate | solution.py:161
  0.7 0.7 %broadcast_in_dim.24 = bf16[16,8,1024]{2,1,0:T(8,128)(2,1)} broadcast(bf16[8,1024]{1,0:T(8,128)(2,1)S(1)} %pad_maximum_fusion.2), dimensions={1,2} | broadcast | bytes 278528 | tf_op jit(solution)/shard_map/broadcast_in_dim | solution.py:164
  1.5 8.3 %all-to-all-start = ((bf16[16,8,1024]{2,1,0:T(8,128)(2,1)}), bf16[16,8,1024]{2,1,0:T(8,128)(2,1)S(1)}, u32[]{:S(2)}, u32[]{:S(2)}) async-start(bf16[16,8,1024]{2,1,0:T(8,128)(2,1)} %broadcast_in_dim.24), calls=%async_computation | async-start | bytes 524288 | tf_op jit(solution)/shard_map/all_to_all | solution.py:163
  9.8 1.1 %fusion.1 = (bf16[128,512]{1,0:T(8,128)(2,1)S(1)}, bf16[128,512]{1,0:T(8,128)(2,1)S(1)}, bf16[128,512]{1,0:T(8,128)(2,1)S(1)}, bf16[128,512]{1,0:T(8,128)(2,1)S(1)}) fusion(bf16[256,512]{1,0:T(8,128)(2,1)} %param.8, bf16[256,512]{1,0:T(8,128)(2,1)} %param.9), kind=kLoop, calls=%fused_computation.9 | loop fusion | bytes 1048576 | tf_op jit(solution)/shard_map/split | solution.py:171
  10.9 0.7 %convert_element_type.6 = bf16[2,2]{1,0:T(2,128)(2,1)S(1)} convert(s32[2,2]{1,0:T(2,128)} %param.12) | non-fusion elementwise | flops 4 | bytes 24 | tf_op jit(solution)/shard_map/convert_element_type | solution.py:173
  11.7 0.1 broadcast_select_fusion
  11.8 0.1 collective-permute-start.2
  11.8 0.7 %collective-permute-start = (bf16[272,512]{1,0:T(8,128)(2,1)S(1)}, bf16[272,512]{1,0:T(8,128)(2,1)S(1)}, u32[]{:S(2)}, u32[]{:S(2)}) collective-permute-start(bf16[272,512]{1,0:T(8,128)(2,1)S(1)} %get-tuple-element.26.far_sent_ref), channel_id=1, source_target_pairs={{1,2},{3,4},{5,6},{7,8},{9,10},{11,12},{13,14},{15,16},{17,18},{19... | collective-permute-start | bytes 835592 | tf_op jit(solution)/shard_map/ppermute | solution.py:182
  12.5 7.9 %all-to-all-done.same_ref = bf16[16,8,1024]{2,1,0:T(8,128)(2,1)S(1)} async-done(((bf16[16,8,1024]{2,1,0:T(8,128)(2,1)}), bf16[16,8,1024]{2,1,0:T(8,128)(2,1)S(1)}, u32[]{:S(2)}, u32[]{:S(2)}) %all-to-all-start) | async-done | bytes 262176 | tf_op jit(solution)/shard_map/all_to_all | solution.py:163
  20.5 0.0 collective-permute-start.1
  20.5 0.7 %pad_add_fusion.meta_ref = s32[4]{0:T(128)S(1)} fusion(s32[2]{0:T(128)} %param.13, s32[1]{0:T(128)} %bitcast.1, s32[1]{0:T(128)} %bitcast), kind=kLoop, calls=%fused_computation.7 | loop fusion | flops 8 | bytes 32 | tf_op jit(solution)/shard_map/concatenate | solution.py:189
  21.2 1.1 %fusion = (bf16[256,512]{1,0:T(8,128)(2,1)S(1)}, bf16[256,512]{1,0:T(8,128)(2,1)S(1)}) fusion(bf16[512,512]{1,0:T(8,128)(2,1)} %param.14), kind=kLoop, calls=%fused_computation.8 | loop fusion | bytes 1048576 | tf_op jit(solution)/shard_map/split | solution.py:186
  22.3 0.0 collective-permute-done.2.near_ref
  22.3 0.0 collective-permute-done.1.other_ref
  22.3 5.2 %inner.1 = (bf16[128,512]{1,0:T(8,128)(2,1)S(1)}, f32[128,512]{1,0:T(8,128)S(1)}) custom-call(s32[4]{0:T(128)S(1)} %pad_add_fusion.meta_ref, bf16[272,512]{1,0:T(8,128)(2,1)S(1)} %collective-permute-done.2.near_ref, bf16[272,512]{1,0:T(8,128)(2,1)S(1)} %get-tuple-element.25.near_sent_ref, bf16[272,512]{1,0:T(8,128)(2,1)S(1)} %get-tuple-element.26.far_sent_ref, ...), custom_call_target="tpu_custom_call" | custom-call | flops 1610612736 | bytes 4718592 | tf_op jit(solution)/shard_map/inner/pallas_call | solution.py:197
  27.5 0.0 collective-permute-done.far_ref
  27.5 3.8 %outer.1 = bf16[256,512]{1,0:T(8,128)(2,1)} custom-call(s32[4]{0:T(128)S(1)} %pad_add_fusion.meta_ref, bf16[272,512]{1,0:T(8,128)(2,1)S(1)} %collective-permute-done.far_ref, bf16[16,8,1024]{2,1,0:T(8,128)(2,1)S(1)} %all-to-all-done.same_ref, bf16[16,8,1024]{2,1,0:T(8,128)(2,1)S(1)} %collective-permute-done.1.other_ref, ...), custom_call_target="tpu_custom_call" | custom-call | flops 402653184 | bytes 2359296 | tf_op jit(solution)/shard_map/outer/pallas_call | solution.py:217
  (3 shorter events, 0.0 us)
Async XLA Ops:
  1.5 19.0 %all-to-all-start = ((bf16[16,8,1024]{2,1,0:T(8,128)(2,1)}), bf16[16,8,1024]{2,1,0:T(8,128)(2,1)S(1)}, u32[]{:S(2)}, u32[]{:S(2)}) async-start(bf16[16,8,1024]{2,1,0:T(8,128)(2,1)} %broadcast_in_dim.24), calls=%async_computation | async-start | bytes 524288 | tf_op jit(solution)/shard_map/all_to_all | solution.py:163
  11.8 10.5 %collective-permute-start.2 = (bf16[272,512]{1,0:T(8,128)(2,1)S(1)}, bf16[272,512]{1,0:T(8,128)(2,1)S(1)}, u32[]{:S(2)}, u32[]{:S(2)}) collective-permute-start(bf16[272,512]{1,0:T(8,128)(2,1)S(1)} %get-tuple-element.25.near_sent_ref), channel_id=1, source_target_pairs={{0,1},{1,0},{2,3},{3,2},{4,5},{5,4},{6,7},{7,6},{8,9},{9,8},{10,11... | collective-permute-start | bytes 835592 | tf_op jit(solution)/shard_map/ppermute | solution.py:183
  11.8 15.6 %collective-permute-start = (bf16[272,512]{1,0:T(8,128)(2,1)S(1)}, bf16[272,512]{1,0:T(8,128)(2,1)S(1)}, u32[]{:S(2)}, u32[]{:S(2)}) collective-permute-start(bf16[272,512]{1,0:T(8,128)(2,1)S(1)} %get-tuple-element.26.far_sent_ref), channel_id=1, source_target_pairs={{1,2},{3,4},{5,6},{7,8},{9,10},{11,12},{13,14},{15,16},{17,18},{19... | collective-permute-start | bytes 835592 | tf_op jit(solution)/shard_map/ppermute | solution.py:182
  20.5 1.8 %collective-permute-start.1 = (bf16[16,8,1024]{2,1,0:T(8,128)(2,1)S(1)}, bf16[16,8,1024]{2,1,0:T(8,128)(2,1)S(1)}, u32[]{:S(2)}, u32[]{:S(2)}) collective-permute-start(bf16[16,8,1024]{2,1,0:T(8,128)(2,1)S(1)} %all-to-all-done.same_ref), channel_id=1, source_target_pairs={{0,1},{1,0},{2,3},{3,2},{4,5},{5,4},{6,7},{7,6},{8,9},{9,8},{10,11... | collective-permute-start | bytes 786440 | tf_op jit(solution)/shard_map/ppermute | solution.py:184
